TPU v7x, 32 devices: a whole 2x2x4 slice. The times are simulated.
32 devices in a mesh: geom: 2 (over x), edge: 4 (over y, core), mode: 4 (over z).
Axes of the slice: x: 2, y: 2, z: 4, core: 2. Of those that a mesh axis runs over, the one named last changes fastest.
Arguments:
- basis: bfloat16 [12288, 1024], P(('geom', 'edge'), 'mode'), parts along dimension 0, may hold values from -6 to 6
- motional: bfloat16 [4, 48, 16, 128, 128], P('geom', 'edge'), parts along dimension 0, may hold values from -0.0017089844 to 0.0017089844
- block_cols: int32 [96, 16], P(('geom', 'edge')), parts along dimension 0, may hold values from 0 to 47, as said below
- block_counts: int32 [96], P(('geom', 'edge')), parts along dimension 0, may hold values from 8 to 16, as said below
Outputs:
- reduced: float32 [4, 1024, 1024], P('geom', 'edge', 'mode'), parts along dimension 0
There are 2 independent parts, one for each index of `geom`. A program takes and returns all parts, laid end to end along the dimension named above; each array names one. Nothing has to cross between parts.
Inputs may be any that keep to these rules, and one draw needn't show every extreme that they name: `block_cols`: block row r's live slots hold distinct block columns within 12 blocks of r (at most r + 12, at least r - 12); slot 0 is r itself; slots at or past block_counts[r] hold r. block_counts[r] never exceeds the number of block columns within 12 blocks of r.
All inputs are finite; a program needn't handle non-finite values.
Results may differ from a plain program's by a relative error of at most 0.0029.
Values may be sent and summed in bfloat16 or wider, within the bound.
A program may use at most 64 MiB of HBM per device.

v0:
```python
import jax
import jax.numpy as jnp
from jax import lax
from jax.sharding import PartitionSpec as P


def padded(x, sides, width):
    for axis, dim in sides:
        size, length = (lax.axis_size(axis), x.shape[dim])
        up = [(i, (i + 1) % size) for i in range(size - 1)]
        down = [(j, i) for i, j in up]
        last = lax.slice_in_dim(x, length - width, length, axis=dim)
        initial = lax.slice_in_dim(x, 0, width, axis=dim)
        before = lax.ppermute(last, axis, up)
        after = lax.ppermute(initial, axis, down)
        x = jnp.concatenate([before, x, after], axis=dim)
    return x


def per_device(basis, motional, block_cols, block_counts):
    rows, cols_local = basis.shape
    nbr, nnz = block_cols.shape
    bsize = motional.shape[-1]
    extended = padded(basis, (("edge", 0),), nbr * bsize)
    tiles = extended.reshape(3 * nbr, bsize, cols_local)
    first_block = lax.axis_index("edge") * nbr
    local_cols = block_cols - first_block + nbr
    live = jnp.arange(nnz, dtype=jnp.int32)[None, :] < block_counts[:, None]
    picked = jnp.take(tiles, local_cols, axis=0)
    picked = jnp.where(live[:, :, None, None], picked, jnp.zeros_like(picked))
    work = jnp.einsum("qbkij,bkjm->qbim", motional, picked, preferred_element_type=jnp.float32)
    work = work.astype(jnp.bfloat16).reshape(2, rows, cols_local)
    partial_sum = jnp.einsum(
        "ri,qrj->qij",
        lax.all_gather(basis, "mode", axis=1, tiled=True),
        work,
        preferred_element_type=jnp.float32,
    )
    total = lax.psum(partial_sum, "edge")
    share = total.shape[1] // lax.axis_size("edge")
    return lax.dynamic_slice_in_dim(total, lax.axis_index("edge") * share, share, 1)


def solution(mesh):
    placed = (
        P(("geom", "edge"), "mode"),
        P("geom", "edge", None, None, None),
        P(("geom", "edge"), None),
        P(("geom", "edge")),
    )
    return jax.shard_map(
        per_device, mesh=mesh, in_specs=placed, out_specs=P("geom", "edge", "mode"), check_vma=False
    )
```

profile of v0, /device:TPU:0, one launch (start us, length us, event | category | flops | bytes accessed | tf_op | source)
XLA Modules:
  0.0 138.8 jit_solution(16012564998397765538)
XLA Ops:
  6.5 0.0 all-gather.2.cloned.1.call-start
  6.5 0.7 all-gather.2.cloned.1.call-update
  7.3 0.0 all-reduce.2.cloned.1.call-start
  7.3 2.4 %collective-permute-start = (bf16[1536,256]{1,0:T(8,128)(2,1)}, bf16[1536,256]{1,0:T(8,128)(2,1)S(1)}, u32[]{:S(2)}, u32[]{:S(2)}) collective-permute-start(bf16[1536,256]{1,0:T(8,128)(2,1)} %param.4), channel_id=1, source_target_pairs={{0,4},{4,8},{8,12},{1,5},{5,9},{9,13},{2,6},{6,10},{10,14},{3,7},{... | collective-permute-start | bytes 2359304 | tf_op jit(solution)/shard_map/ppermute | solution.py:14
  9.7 1.3 collective-permute-start.1
  11.0 0.8 compare_and_fusion
  11.8 0.1 reshape.36
  11.9 0.0 collective-permute-done
  11.9 4.4 %collective-permute-done.1 = bf16[1536,256]{1,0:T(8,128)(2,1)} collective-permute-done((bf16[1536,256]{1,0:T(8,128)(2,1)}, bf16[1536,256]{1,0:T(8,128)(2,1)}, u32[]{:S(2)}, u32[]{:S(2)}) %collective-permute-start.1) | collective-permute-done | bytes 786464 | tf_op jit(solution)/shard_map/ppermute | solution.py:15
  16.3 1.5 %pad_maximum_fusion = bf16[4608,256]{1,0:T(8,128)(2,1)S(1)} fusion(bf16[1536,256]{1,0:T(8,128)(2,1)} %collective-permute-done.1, bf16[1536,256]{1,0:T(8,128)(2,1)} %param.4, bf16[1536,256]{1,0:T(8,128)(2,1)S(1)} %collective-permute-done), kind=kLoop, calls=%fused_computation.13 | loop fusion | flops 7077888 | bytes 4718592 | tf_op jit(solution)/shard_map/concatenate | solution.py:16
  17.9 8.2 %gather_fusion = bf16[192,128,256]{2,1,0:T(8,128)(2,1)} fusion(bf16[36,128,256]{2,1,0:T(8,128)(2,1)S(1)} %bitcast.27, s32[1024]{0:T(1024)S(1)} %pad_clamp_fusion), kind=kCustom, calls=%fused_computation | custom fusion | bytes 25166592 | tf_op jit(solution)/shard_map/jit(_take)/gather | solution.py:29
  26.1 10.5 %fusion.18 = bf16[2,12,128,256]{3,2,0,1:T(8,128)(2,1)S(1)} fusion(bf16[2,12,16,128,128]{4,3,2,1,0:T(8,128)(2,1)} %param.5, bf16[12,16,128,256]{3,2,1,0:T(8,128)(2,1)} %bitcast.28, pred[12,16]{1,0:T(8,128)(4,1)S(1)} %get-tuple-element.5, pred[12,16]{1,0:T(8,128)(4,1)S(1)} %get-tuple-element.7), kind=kOutput, calls=%fused_computation.15 | convolution fusion | flops 3234594816 | bytes 26739072 | tf_op jit(solution)/shard_map/qbkij,bkjm->qbim/dot_general | solution.py:31
  36.5 0.1 copy.8
  36.7 38.4 %all-gather.2.cloned.1.call-done = bf16[1536,1024]{1,0:T(8,128)(2,1)} async-done(((bf16[1536,256]{1,0:T(8,128)(2,1)}), bf16[1536,1024]{1,0:T(8,128)(2,1)}) %all-gather.2.cloned.1.call-update) | async-done | bytes 3145744 | tf_op jit(solution)/shard_map/all_gather | solution.py:35
  75.1 5.0 %fusion.15 = f32[2,1024,256]{1,2,0:T(8,128)} fusion(bf16[2,1536,256]{2,1,0:T(8,128)(2,1)S(1)} %bitcast.29, bf16[1536,1024]{1,0:T(8,128)(2,1)} %all-gather.2.cloned.1.call-done), kind=kOutput, calls=%fused_computation.14 | convolution fusion | flops 1610612736 | bytes 6815744 | tf_op jit(solution)/shard_map/ri,qrj->qij/dot_general | solution.py:33
  80.1 0.0 all-reduce.2.cloned.1.call-update
  80.2 49.7 %all-reduce.2.cloned.1.call-done = f32[2,1024,256]{1,2,0:T(8,128)} async-done(((f32[2,1024,256]{1,2,0:T(8,128)}), f32[2,1024,256]{1,2,0:T(8,128)}) %all-reduce.2.cloned.1.call-update) | async-done | bytes 2097168 | tf_op jit(solution)/shard_map/psum | solution.py:39
  129.9 1.1 constant_dynamic-slice_fusion
  130.9 1.0 copy.10
  (1 shorter events, 0.0 us)
Async XLA Ops:
  6.5 68.5 %all-gather.2.cloned.1.call-start = ((), (), s32[]{:S(2)}) async-start(), calls=%async_computation | async-start | bytes 3932160 | tf_op jit(solution)/shard_map/all_gather | solution.py:35
  7.3 122.6 %all-reduce.2.cloned.1.call-start = ((), (), s32[]{:S(2)}) async-start(), calls=%async_computation.1 | async-start | bytes 4194304 | tf_op jit(solution)/shard_map/psum | solution.py:39
  7.3 4.6 %collective-permute-start = (bf16[1536,256]{1,0:T(8,128)(2,1)}, bf16[1536,256]{1,0:T(8,128)(2,1)S(1)}, u32[]{:S(2)}, u32[]{:S(2)}) collective-permute-start(bf16[1536,256]{1,0:T(8,128)(2,1)} %param.4), channel_id=1, source_target_pairs={{0,4},{4,8},{8,12},{1,5},{5,9},{9,13},{2,6},{6,10},{10,14},{3,7},{... | collective-permute-start | bytes 2359304 | tf_op jit(solution)/shard_map/ppermute | solution.py:14
  9.7 6.6 %collective-permute-start.1 = (bf16[1536,256]{1,0:T(8,128)(2,1)}, bf16[1536,256]{1,0:T(8,128)(2,1)}, u32[]{:S(2)}, u32[]{:S(2)}) collective-permute-start(bf16[1536,256]{1,0:T(8,128)(2,1)} %param.4), channel_id=1, source_target_pairs={{4,0},{8,4},{12,8},{5,1},{9,5},{13,9},{6,2},{10,6},{14,10},{7,3},{... | collective-permute-start | bytes 2359304 | tf_op jit(solution)/shard_map/ppermute | solution.py:15
Sparse Core Ops, SparseCore 0:
  8.9 66.1 all-gather.1
  80.3 49.5 all-reduce.1
where the time goes:
time: 139 us
  waiting for transfers between devices  93.2 us (67%)
  matrix products  15.5 us (11%)
  between operations  13.5 us (10%)
  local copies, waits for them, and re-layouts  10.5 us (8%)
  starting transfers between devices  3.74 us (3%)
  other arithmetic  2.31 us (2%)
    psum x1, waiting for transfers between devices, per_device(): total = lax.psum(partial_sum, 'edge')  49.7 us
    all_gather x1, waiting for transfers between devices, per_device(): lax.all_gather(basis, 'mode', axis=1, tiled=True)  38.4 us
    dot_general x1, matrix products, per_device(): jnp.einsum('qbkij,bkjm->qbim', motional, picked, preferred_element_type=j...  10.5 us
    gather x1, local copies, waits for them, and re-layouts, per_device(): picked = jnp.take(tiles, local_cols, axis=0)  8.2 us
    dot_general x1, matrix products, per_device(): jnp.einsum('ri,qrj->qij', lax.all_gather(basis, 'mode', axis=1, tiled=Tru...  5.05 us
    ppermute x1, waiting for transfers between devices, padded(): after = lax.ppermute(initial, axis, down)  4.43 us
  transfers between devices with their start and end apart: 4, of which 3 were waited for; matrix products, arithmetic and copies ran while one was open for 15% of the time, Pallas kernels for 0%

commit v1 on v0

--- a/solution.py
+++ b/solution.py
@@ -2,6 +2,12 @@
 import jax.numpy as jnp
 from jax import lax
 from jax.sharding import PartitionSpec as P
+
+
+def joined_along(blocks, dim):
+    blocks = jnp.moveaxis(blocks, 0, dim)
+    shape = blocks.shape
+    return blocks.reshape(*shape[:dim], shape[dim] * shape[dim + 1], *shape[dim + 2 :])
 
 
 def padded(x, sides, width):
@@ -30,12 +36,16 @@
     picked = jnp.where(live[:, :, None, None], picked, jnp.zeros_like(picked))
     work = jnp.einsum("qbkij,bkjm->qbim", motional, picked, preferred_element_type=jnp.float32)
     work = work.astype(jnp.bfloat16).reshape(2, rows, cols_local)
-    partial_sum = jnp.einsum(
-        "ri,qrj->qij",
-        lax.all_gather(basis, "mode", axis=1, tiled=True),
-        work,
-        preferred_element_type=jnp.float32,
-    )
+    size_2, index, rows_2 = (lax.axis_size("mode"), lax.axis_index("mode"), basis.shape[1])
+    ahead = [(i_2, (i_2 + 1) % size_2) for i_2 in range(size_2)]
+    blocks = []
+    current = basis
+    for step in range(size_2):
+        coming = current if step == size_2 - 1 else lax.ppermute(current, "mode", ahead)
+        blocks.append(jnp.einsum("ri,qrj->qij", current, work, preferred_element_type=jnp.float32))
+        current = coming
+    blocks = jnp.stack(blocks)[(index - jnp.arange(size_2)) % size_2]
+    partial_sum = joined_along(blocks, 1)
     total = lax.psum(partial_sum, "edge")
     share = total.shape[1] // lax.axis_size("edge")
     return lax.dynamic_slice_in_dim(total, lax.axis_index("edge") * share, share, 1)

time: 139 us -> 139 us (level)
  waiting for transfers between devices: 93.2 us -> 86.7 us
  local copies, waits for them, and re-layouts: 10.5 us -> 15.2 us
  starting transfers between devices: 3.74 us -> 6.43 us
  matrix products: 15.5 us -> 14 us
    all_gather x1 -> x0, waiting for transfers between devices: 38.4 us -> none  [per_device(): lax.all_gather(basis, 'mode', axis=1, tiled=True)]
    ppermute x0 -> x3, waiting for transfers between devices: none -> 33 us  [per_device(): lax.ppermute(current, 'mode', ahead)]
    transpose x0 -> x1, local copies, waits for them, and re-layouts: none -> 2.95 us  [joined_along(): blocks = jnp.moveaxis(blocks, 0, dim)]
    ppermute x0 -> x3, starting transfers between devices: none -> 2.74 us  [per_device(): lax.ppermute(current, 'mode', ahead)]
    ppermute x1, waiting for transfers between devices: 4.43 us -> 1.95 us  [padded(): after = lax.ppermute(initial, axis, down)]
    psum x1, waiting for transfers between devices: 49.7 us -> 51.8 us  [per_device(): total = lax.psum(partial_sum, 'edge')]
    gather x0 -> x1, local copies, waits for them, and re-layouts: none -> 1.99 us  [per_device(): blocks = jnp.stack(blocks)[(index - jnp.arange(size_2)) % size_2]]
    dot_general x1 -> x4, matrix products: 5.05 us -> 3.57 us  [per_device(): jnp.einsum('ri,qrj->qij', current, work, preferred_element_type=jnp.float32)]
  transfers between devices with their start and end apart: 4 -> 6, of which waited for: 3 -> 5; matrix products, arithmetic and copies ran while one was open for 15% -> 17% of each run, Pallas kernels for 0% -> 0%
where the time goes in v1:
time: 139 us; the launch traced here: 138 us
  waiting for transfers between devices  86.7 us (62%)
  local copies, waits for them, and re-layouts  15.2 us (11%)
  matrix products  14 us (10%)
  between operations  13.5 us (10%)
  starting transfers between devices  6.43 us (5%)
  other arithmetic  2.55 us (2%)
    psum x1, waiting for transfers between devices, per_device(): total = lax.psum(partial_sum, 'edge')  51.8 us
    ppermute x3, waiting for transfers between devices, per_device(): lax.ppermute(current, 'mode', ahead)  33 us
    dot_general x1, matrix products, per_device(): jnp.einsum('qbkij,bkjm->qbim', motional, picked, preferred_element_type=j...  10.4 us
    gather x1, local copies, waits for them, and re-layouts, per_device(): picked = jnp.take(tiles, local_cols, axis=0)  8.19 us
    dot_general x4, matrix products, per_device(): jnp.einsum('ri,qrj->qij', current, work, preferred_element_type=jnp.float32)  3.57 us
    transpose x1, local copies, waits for them, and re-layouts, joined_along(): blocks = jnp.moveaxis(blocks, 0, dim)  2.95 us
  transfers between devices with their start and end apart: 6, of which 5 were waited for; matrix products, arithmetic and copies ran while one was open for 17% of the time, Pallas kernels for 0%

profile of v1, /device:TPU:0, one launch (start us, length us, event | category | flops | bytes accessed | tf_op | source)
XLA Modules:
  0.0 138.4 jit_solution(8554068915400932479)
XLA Ops:
  6.5 0.0 all-reduce.2.cloned.1.call-start
  6.5 2.4 %collective-permute-start = (bf16[1536,256]{1,0:T(8,128)(2,1)}, bf16[1536,256]{1,0:T(8,128)(2,1)S(1)}, u32[]{:S(2)}, u32[]{:S(2)}) collective-permute-start(bf16[1536,256]{1,0:T(8,128)(2,1)} %param.4), channel_id=1, source_target_pairs={{0,4},{4,8},{8,12},{1,5},{5,9},{9,13},{2,6},{6,10},{10,14},{3,7},{... | collective-permute-start | bytes 2359304 | tf_op jit(solution)/shard_map/ppermute | solution.py:20
  8.9 1.3 collective-permute-start.1
  10.2 2.5 %collective-permute-start.2 = (bf16[1536,256]{1,0:T(8,128)(2,1)}, bf16[1536,256]{1,0:T(8,128)(2,1)}, u32[]{:S(2)}, u32[]{:S(2)}) collective-permute-start(bf16[1536,256]{1,0:T(8,128)(2,1)} %param.4), channel_id=1, source_target_pairs={{0,1},{1,2},{2,3},{3,0},{4,5},{5,6},{6,7},{7,4},{8,9},{9,10},{10,1... | collective-permute-start | bytes 2359304 | tf_op jit(solution)/shard_map/ppermute | solution.py:44
  12.7 0.8 compare_and_fusion
  13.5 0.1 reshape.89
  13.6 0.0 collective-permute-done
  13.6 2.0 %collective-permute-done.1 = bf16[1536,256]{1,0:T(8,128)(2,1)} collective-permute-done((bf16[1536,256]{1,0:T(8,128)(2,1)}, bf16[1536,256]{1,0:T(8,128)(2,1)}, u32[]{:S(2)}, u32[]{:S(2)}) %collective-permute-start.1) | collective-permute-done | bytes 786464 | tf_op jit(solution)/shard_map/ppermute | solution.py:21
  15.6 1.5 %pad_maximum_fusion = bf16[4608,256]{1,0:T(8,128)(2,1)S(1)} fusion(bf16[1536,256]{1,0:T(8,128)(2,1)} %collective-permute-done.1, bf16[1536,256]{1,0:T(8,128)(2,1)} %param.4, bf16[1536,256]{1,0:T(8,128)(2,1)S(1)} %collective-permute-done), kind=kLoop, calls=%fused_computation.12 | loop fusion | flops 7077888 | bytes 4718592 | tf_op jit(solution)/shard_map/concatenate | solution.py:22
  17.1 8.2 %gather_fusion = bf16[192,128,256]{2,1,0:T(8,128)(2,1)} fusion(bf16[36,128,256]{2,1,0:T(8,128)(2,1)S(1)} %bitcast.55, s32[1024]{0:T(1024)S(1)} %pad_clamp_fusion.1), kind=kCustom, calls=%fused_computation | custom fusion | bytes 25166592 | tf_op jit(solution)/shard_map/jit(_take)/gather | solution.py:35
  25.3 6.4 %collective-permute-done.2 = bf16[1536,256]{1,0:T(8,128)(2,1)} collective-permute-done((bf16[1536,256]{1,0:T(8,128)(2,1)}, bf16[1536,256]{1,0:T(8,128)(2,1)}, u32[]{:S(2)}, u32[]{:S(2)}) %collective-permute-start.2) | collective-permute-done | bytes 786464 | tf_op jit(solution)/shard_map/ppermute | solution.py:44
  31.7 0.3 collective-permute-start.3
  32.0 10.4 %fusion.13 = bf16[2,12,128,256]{3,2,0,1:T(8,128)(2,1)S(1)} fusion(bf16[2,12,16,128,128]{4,3,2,1,0:T(8,128)(2,1)} %param.5, bf16[12,16,128,256]{3,2,1,0:T(8,128)(2,1)} %bitcast.56, pred[12,16]{1,0:T(8,128)(4,1)S(1)} %get-tuple-element.5, pred[12,16]{1,0:T(8,128)(4,1)S(1)} %get-tuple-element.7), kind=kOutput, calls=%fused_computation.14 | convolution fusion | flops 3234594816 | bytes 26739072 | tf_op jit(solution)/shard_map/qbkij,bkjm->qbim/dot_general | solution.py:37
  42.4 0.0 copy-start
  42.4 0.1 copy.7
  42.5 8.9 %collective-permute-done.3 = bf16[1536,256]{1,0:T(8,128)(2,1)S(1)} collective-permute-done((bf16[1536,256]{1,0:T(8,128)(2,1)}, bf16[1536,256]{1,0:T(8,128)(2,1)S(1)}, u32[]{:S(2)}, u32[]{:S(2)}) %collective-permute-start.3) | collective-permute-done | bytes 786464 | tf_op jit(solution)/shard_map/ppermute | solution.py:44
  51.4 0.0 collective-permute-start.4
  51.4 0.0 copy-done
  51.4 0.6 convolution_bitcast_fusion.3
  52.1 1.7 %convolution_bitcast_fusion.2 = f32[1,2,256,256]{2,3,1,0:T(8,128)S(1)} fusion(bf16[2,1536,256]{2,1,0:T(8,128)(2,1)S(1)} %bitcast.60, bf16[1536,256]{1,0:T(8,128)(2,1)} %collective-permute-done.2), kind=kOutput, calls=%fused_computation.17 | convolution fusion | flops 402653184 | bytes 2883584 | tf_op jit(solution)/shard_map/ri,qrj->qij/dot_general | solution.py:45
  53.8 0.6 convolution_bitcast_fusion.1
  54.4 17.6 %collective-permute-done.4 = bf16[1536,256]{1,0:T(8,128)(2,1)S(1)} collective-permute-done((bf16[1536,256]{1,0:T(8,128)(2,1)S(1)}, bf16[1536,256]{1,0:T(8,128)(2,1)S(1)}, u32[]{:S(2)}, u32[]{:S(2)}) %collective-permute-start.4) | collective-permute-done | bytes 786464 | tf_op jit(solution)/shard_map/ppermute | solution.py:44
  72.1 0.6 convolution_bitcast_fusion
  72.7 0.2 pad_maximum_fusion.1
  72.9 2.0 %gather_fusion.1 = f32[4,2,256,256]{2,3,1,0:T(8,128)} fusion(f32[4,2,256,256]{2,3,1,0:T(8,128)S(1)} %pad_maximum_fusion.1, s32[1024]{0:T(1024)S(1)} %pad_clamp_fusion), kind=kCustom, calls=%fused_computation.1 | custom fusion | bytes 4194320 | tf_op jit(solution)/shard_map/gather | solution.py:47
  74.9 2.9 %copy.12 = f32[2,4,256,256]{3,2,1,0:T(8,128)} copy(f32[2,4,256,256]{2,3,0,1:T(8,128)} %bitcast.58) | data formatting | bytes 4194304 | tf_op jit(solution)/shard_map/transpose | solution.py:8
  77.8 0.0 all-reduce.2.cloned.1.call-update
  77.9 51.8 %all-reduce.2.cloned.1.call-done = f32[2,1024,256]{2,1,0:T(8,128)} async-done(((f32[2,1024,256]{2,1,0:T(8,128)}), f32[2,1024,256]{2,1,0:T(8,128)}) %all-reduce.2.cloned.1.call-update) | async-done | bytes 2097168 | tf_op jit(solution)/shard_map/psum | solution.py:49
  129.7 1.9 %constant_dynamic-slice_fusion = f32[2,256,256]{2,1,0:T(8,128)} fusion(f32[2,1024,256]{2,1,0:T(8,128)} %all-reduce.2.cloned.1.call-done, s32[]{:T(128)S(6)} %select_n.45), kind=kLoop, calls=%fused_computation.34 | loop fusion | bytes 1048580 | tf_op jit(solution)/shard_map/dynamic_slice | solution.py:51
  (3 shorter events, 0.0 us)
Async XLA Ops:
  6.5 123.2 %all-reduce.2.cloned.1.call-start = ((), (), s32[]{:S(2)}) async-start(), calls=%async_computation | async-start | bytes 4194304 | tf_op jit(solution)/shard_map/psum | solution.py:49
  6.5 7.1 %collective-permute-start = (bf16[1536,256]{1,0:T(8,128)(2,1)}, bf16[1536,256]{1,0:T(8,128)(2,1)S(1)}, u32[]{:S(2)}, u32[]{:S(2)}) collective-permute-start(bf16[1536,256]{1,0:T(8,128)(2,1)} %param.4), channel_id=1, source_target_pairs={{0,4},{4,8},{8,12},{1,5},{5,9},{9,13},{2,6},{6,10},{10,14},{3,7},{... | collective-permute-start | bytes 2359304 | tf_op jit(solution)/shard_map/ppermute | solution.py:20
  8.9 6.6 %collective-permute-start.1 = (bf16[1536,256]{1,0:T(8,128)(2,1)}, bf16[1536,256]{1,0:T(8,128)(2,1)}, u32[]{:S(2)}, u32[]{:S(2)}) collective-permute-start(bf16[1536,256]{1,0:T(8,128)(2,1)} %param.4), channel_id=1, source_target_pairs={{4,0},{8,4},{12,8},{5,1},{9,5},{13,9},{6,2},{10,6},{14,10},{7,3},{... | collective-permute-start | bytes 2359304 | tf_op jit(solution)/shard_map/ppermute | solution.py:21
  10.2 21.4 %collective-permute-start.2 = (bf16[1536,256]{1,0:T(8,128)(2,1)}, bf16[1536,256]{1,0:T(8,128)(2,1)}, u32[]{:S(2)}, u32[]{:S(2)}) collective-permute-start(bf16[1536,256]{1,0:T(8,128)(2,1)} %param.4), channel_id=1, source_target_pairs={{0,1},{1,2},{2,3},{3,0},{4,5},{5,6},{6,7},{7,4},{8,9},{9,10},{10,1... | collective-permute-start | bytes 2359304 | tf_op jit(solution)/shard_map/ppermute | solution.py:44
  31.7 19.8 %collective-permute-start.3 = (bf16[1536,256]{1,0:T(8,128)(2,1)}, bf16[1536,256]{1,0:T(8,128)(2,1)S(1)}, u32[]{:S(2)}, u32[]{:S(2)}) collective-permute-start(bf16[1536,256]{1,0:T(8,128)(2,1)} %collective-permute-done.2), channel_id=1, source_target_pairs={{0,1},{1,2},{2,3},{3,0},{4,5},{5,6},{6,7},{7,4},{8,9},{9,10},{10,1... | collective-permute-start | bytes 2359304 | tf_op jit(solution)/shard_map/ppermute | solution.py:44
  42.4 9.0 %copy-start = (bf16[1536,256]{1,0:T(8,128)(2,1)S(1)}, bf16[1536,256]{1,0:T(8,128)(2,1)}, u32[]{:S(2)}) copy-start(bf16[1536,256]{1,0:T(8,128)(2,1)} %param.4) | copy-start | bytes 2359300
  51.4 20.6 %collective-permute-start.4 = (bf16[1536,256]{1,0:T(8,128)(2,1)S(1)}, bf16[1536,256]{1,0:T(8,128)(2,1)S(1)}, u32[]{:S(2)}, u32[]{:S(2)}) collective-permute-start(bf16[1536,256]{1,0:T(8,128)(2,1)S(1)} %collective-permute-done.3), channel_id=1, source_target_pairs={{0,1},{1,2},{2,3},{3,0},{4,5},{5,6},{6,7},{7,4},{8,9},{9,10},{10,1... | collective-permute-start | bytes 2359304 | tf_op jit(solution)/shard_map/ppermute | solution.py:44
Sparse Core Ops, SparseCore 0:
  78.0 51.6 all-reduce.1
